TPU v7x, 32 devices: a whole 2x2x4 slice. The times are simulated.
32 devices in a mesh: space: 8 (over y, x, core), lane: 4 (over z).
Axes of the slice: x: 2, y: 2, z: 4, core: 2. Of those that a mesh axis runs over, the one named last changes fastest.
Arguments:
- positions: float32 [256, 3, 544], P('space'), may hold values from -6 to 6
- bend_op: float32 [544, 544], replicated, may hold values from -0.25 to 0.25
- send_list: int32 [8, 8], P('space'), may hold values from 0 to 31
- task_target: int32 [32, 12], P(('space', 'lane')), may hold values from 0 to 31, as said below
- task_source: int32 [32, 12], P(('space', 'lane')), may hold values from 0 to 39, as said below
- task_count: int32 [32], P(('space', 'lane')), may hold values from 4 to 12, as said below
Outputs:
- moved_positions: float32 [256, 3, 544], P(('space', 'lane'))
- velocity: float32 [256, 3, 544], P(('space', 'lane'))
Inputs may be any that keep to these rules, and one draw needn't show every extreme that they name: `task_target`: slots at or beyond the list's task_count hold 0. `task_source`: slots at or beyond the list's task_count hold 0. Every received cell of an owner is the source of at least one live slot of that owner. `task_count`: in each owner exactly one lane has 12 live slots; every other lane has at most 7.
All inputs are finite; a program needn't handle non-finite values.
Results may differ from a plain program's by a relative error of at most 0.00015.
Values sent between devices are 32-bit elements; how exact they have to be, the bound alone decides.
No kernel may reach another device: no remote copies, remote signals or barrier semaphores. Data moves between devices by JAX's collectives and lax.ppermute only.
A program may use at most 64 MiB of HBM per device.

v0:
```python
import functools
from types import SimpleNamespace

import jax
import jax.numpy as jnp
from jax import lax
from jax.experimental import pallas as pl
from jax.experimental.pallas import tpu as pltpu
from jax.sharding import PartitionSpec as P

REGULARIZE = 0.25
TIME_STEP = 0.5
UNROLL = 11
PAIR = 2
SOURCE_ROWS = 24
SUM_ROWS = 16

F32 = jnp.float32
BF16 = jnp.bfloat16
VMEM = pl.BlockSpec(memory_space=pltpu.VMEM)
SMEM = pl.BlockSpec(memory_space=pltpu.SMEM)
HBM = pl.BlockSpec(memory_space=pltpu.HBM)
ANY = pl.BlockSpec(memory_space=pl.ANY)


def up(value, step):
    return -(-value // step) * step


def sizes(owners, lanes, cells, points, cap, listed):
    main = 128 * (points // (128 * lanes))
    rest = (points - main * lanes) // lanes
    group = listed // owners
    pool = up(cells + listed, 8)
    per_pack = 128 // rest
    return SimpleNamespace(
        owners=owners,
        lanes=lanes,
        cells=cells,
        points=points,
        cap=cap,
        group=group,
        width=up(points, 128),
        tiles=up(points, 128) // 128,
        main=main,
        rest=rest,
        rest_tiles=up(rest * lanes, 128) // 128,
        chunk=main + rest,
        chunk_wide=main + up(rest, 128),
        chunk_tiles=(main + up(rest, 128)) // 128,
        per_pack=per_pack,
        pool=pool,
        share=cells // lanes,
        slots=up(lanes * cap + UNROLL, 8),
        rows=cells + 8,
        own=up(lanes * cap + PAIR, 8),
    )


def pack_rows(sz, rows):
    return (3 * rows * sz.main // 128) + 8 * up(3 * rows // 8, sz.per_pack) // sz.per_pack


def split2(value):
    high = value.astype(BF16)
    return high, (value - high.astype(F32)).astype(BF16)


def split3(value):
    first = value.astype(BF16).astype(F32)
    left = value - first
    second = left.astype(BF16).astype(F32)
    return first, second, left - second


def lane_iota(rows):
    return lax.broadcasted_iota(jnp.int32, (rows, 128), 1)


def fetch(sources, targets, sems):
    copies = [
        pltpu.make_async_copy(source, target, sems.at[q])
        for q, (source, target) in enumerate(zip(sources, targets))
    ]
    for copy in copies:
        copy.start()
    return copies


def loop(count, body):
    if count <= 8:
        for q in range(count):
            body(q)
    else:

        def step(q, carry):
            body(q)
            return carry

        lax.fori_loop(0, count, step, 0)


def own_chunk(sz, lane, ref, rows):
    parts = []
    if sz.main:
        parts.append(ref[rows, pl.ds(pl.multiple_of(lane * sz.main, 128), sz.main)])
    start = sz.rest * lane
    lanes = lane_iota(8)
    rest = jnp.zeros((8, 128), F32)
    for tile in range(sz.rest_tiles):
        offset = sz.main * sz.lanes + 128 * tile
        block = ref[rows, offset : min(offset + 128, ref.shape[-1])]
        if block.shape[1] < 128:
            block = jnp.concatenate([block, jnp.zeros((8, 128 - block.shape[1]), F32)], axis=1)
        inside = (lanes + 128 * tile >= start) & (lanes + 128 * tile < start + sz.rest)
        rest = rest + jnp.where(inside, block, 0.0)
    rest = pltpu.roll(rest, lax.rem(128 * sz.rest_tiles - start, 128), 1)
    parts.append(rest)
    return jnp.concatenate(parts, axis=1) if len(parts) > 1 else parts[0]


def send_ghosts(sz, send, chunks, out, tasks):
    lanes = lane_iota(1)

    def one(d):
        for g in range(sz.group):
            cell = send[0, d * sz.group + g]
            rows = []
            last = tasks
            for i in range(3):
                row = chunks[pl.ds(i * sz.rows + cell, 1), :]
                rows.append(row[:, :128] if sz.main else jnp.zeros((1, 128), F32))
                piece = jnp.where(lanes < sz.rest, row[:, sz.main : sz.main + 128], 0.0)
                last = last + (pltpu.roll(piece, i * sz.rest, 1) if i else piece)
            rows.append(last)
            for other in range(sz.lanes):
                first = ((d * sz.lanes + other) * sz.group + g) * 4
                for q, row in enumerate(rows):
                    out[pl.ds(first + q, 1), :] = row

    loop(sz.owners, one)


def pick_kernel(sz, *refs):
    inputs, (out, send_out), held, (chunks, sems) = refs[:5], refs[5:7], refs[7:12], refs[12:]
    for copy in fetch(inputs, held, sems):
        copy.wait()
    send, target, source, count, positions = held
    for j in range(send_out.shape[1]):
        send_out[0, j] = send[0, j]
    lane = lax.axis_index("lane")
    for i in range(3):
        for g in range(0, sz.cells, 8):
            value = own_chunk(sz, lane, positions.at[i], pl.ds(g, 8))
            chunks[pl.ds(i * sz.rows + g, 8), :] = value
    spare = jnp.zeros((1, 128 - sz.cap), F32)
    tasks = jnp.where(lane_iota(1) == 3 * sz.rest + 2 * sz.cap, count[0].astype(F32), 0.0)
    for q, row in enumerate((target, source)):
        wide = jnp.concatenate([row[...].astype(F32), spare], axis=1)
        tasks = tasks + pltpu.roll(wide, 3 * sz.rest + q * sz.cap, 1)
    send_ghosts(sz, send, chunks, out, tasks)


def take_ghosts(sz, arrived, pool, stride, base):
    lanes = lane_iota(1)

    def one(d):
        for g in range(sz.group):
            first = [((d * sz.lanes + lane) * sz.group + g) * 4 for lane in range(sz.lanes)]
            last = [arrived[pl.ds(row + 3, 1), :] for row in first]
            for i in range(3):
                tiles = []
                if sz.main:
                    tiles += [arrived[pl.ds(row + i, 1), :] for row in first]
                for tile in range(sz.rest_tiles):
                    total = jnp.zeros((1, 128), F32)
                    for lane in range(sz.lanes):
                        start = sz.rest * lane
                        if start + sz.rest <= 128 * tile or start >= 128 * tile + 128:
                            continue
                        shift = (start - i * sz.rest) % 128
                        value = pltpu.roll(last[lane], shift, 1) if shift else last[lane]
                        at = lanes + 128 * tile
                        total = jnp.where((at >= start) & (at < start + sz.rest), value, total)
                    tiles.append(total)
                place = pl.ds(i * stride + base + d * sz.group + g, 1)
                pool[place, :] = jnp.concatenate(tiles, axis=1)

    loop(sz.owners, one)


def build_list(sz, lists, tasks):
    total = jnp.int32(0)
    for lane in range(sz.lanes):
        count = lists[lane, 2 * sz.cap]
        for j in range(sz.cap):
            tasks[0, total] = lists[lane, j]
            tasks[1, total] = lists[lane, sz.cap + j]
            total = total + (j < count).astype(jnp.int32)
    for u in range(UNROLL):
        tasks[0, total + u] = jnp.int32(sz.cells)
        tasks[1, total + u] = jnp.int32(0)
    tasks[2, 0] = total
    return total


def own_list(sz, lane, tasks, mine, low, high):
    first = lane * sz.share
    total = tasks[2, 0]
    count = jnp.int32(0)
    for t in range(sz.lanes * sz.cap):
        target = tasks[0, t] - first
        source = tasks[1, t]
        mine[0, count] = target
        mine[1, count] = source - low
        taken = (target >= 0) & (target < sz.share) & (t < total)
        taken = taken & (source >= low) & (source < high)
        count = count + taken.astype(jnp.int32)
    for u in range(PAIR):
        mine[0, count + u] = jnp.int32(-1)
        mine[1, count + u] = jnp.int32(0)
    return count


def products(value, bend_high, bend_low):
    high, low = split2(value)
    dot = functools.partial(jnp.dot, preferred_element_type=F32)
    return dot(high, bend_high) + dot(low, bend_high) + dot(high, bend_low)


def make_sources(sz, value, bend_high, bend_low, source_rows, centres, first):
    count = value.shape[0] // 3
    forces = products(value[:, : sz.points], bend_high, bend_low)
    forces = jnp.concatenate(
        [forces, jnp.zeros((3 * count, sz.width - sz.points), F32)], axis=1
    )
    middle = jnp.sum(value, axis=1, keepdims=True) / sz.points
    for g in range(count // 8):
        where = [i * count + 8 * g for i in range(3)]
        middles = [jnp.broadcast_to(middle[w : w + 8], (8, 128)) for w in where]
        middles += [jnp.zeros((8, 128), F32)] * 5
        for i, row in enumerate(middles):
            centres[pl.ds(8 * (first + 8 * g) + i, 8, stride=8), :] = row
        for j in range(sz.tiles):
            cut = slice(128 * j, 128 * j + 128)
            y = [value[w : w + 8, cut] - m for w, m in zip(where, middles)]
            f = [forces[w : w + 8, cut] for w in where]
            norm = y[0] * y[0] + y[1] * y[1] + y[2] * y[2] + REGULARIZE
            along = y[0] * f[0] + y[1] * f[1] + y[2] * f[2]
            one, zero = jnp.ones((8, 128), F32), jnp.zeros((8, 128), F32)
            rows = [y[0], y[1], y[2], norm, one, zero, zero, zero]
            rows += f
            rows += [y[i] * f[k] for i in range(3) for k in range(3)]
            rows += [norm * f[i] + along * y[i] for i in range(3)]
            rows += [along]
            for k, row in enumerate(rows):
                place = pl.ds(SOURCE_ROWS * (first + 8 * g) + k, 8, stride=SOURCE_ROWS)
                source_rows.at[j][place, :] = row


def make_targets(sz, blocks, targets):
    targets[...] = jnp.zeros_like(targets)
    for i in range(3):
        for g in range(blocks[i].shape[0] // 8):
            block = blocks[i][8 * g : 8 * g + 8]
            for j in range(targets.shape[0]):
                cut = slice(128 * j, 128 * j + 128)
                targets.at[j][pl.ds(64 * g + i, 8, stride=8), :] = block[:, cut]


def source_operands(sz, source, source_rows):
    held = [
        source_rows[j, pl.ds(pl.multiple_of(SOURCE_ROWS * source, 8), SOURCE_ROWS), :]
        for j in range(sz.tiles)
    ]
    held = jnp.concatenate(held, axis=1)
    y1, y2, y3 = split3(held[:8])
    y_stack = jnp.concatenate([y1, y1, y2, y2, y1, y3], axis=0).astype(BF16)
    return y_stack, jnp.concatenate(split3(held[8:]), axis=0)


def pieces(points, step):
    starts = list(range(0, max(points // 128 * 128, 1), step))
    return list(zip(starts, starts[1:] + [points]))


def twice(piece, count):
    whole = count // 128 * 128
    parts = [piece[:, :whole].astype(BF16)] * 2 if whole else []
    if whole < count:
        last = piece[:, whole:]
        last = last + pltpu.roll(last, count - whole, 1)
        parts.append(last.astype(BF16)[:, : 2 * (count - whole)])
    return jnp.concatenate(parts, axis=1)


def load_target(j, target, slot, centre, targets, offsets):
    row = lax.broadcasted_iota(jnp.int32, (8, 128), 0)
    x = targets[j, pl.ds(pl.multiple_of(8 * target, 8), 8), :] - centre
    square = x * x
    norm = pltpu.roll(square, 2, 0) + pltpu.roll(square, 3, 0) + pltpu.roll(square, 4, 0)
    side = jnp.where(row == 4, norm, jnp.where(row == 3, 1.0, 0.0))
    x_side = jnp.where(row < 3, -2.0 * x, side)
    x1, x2, x3 = split3(x_side)
    return x, jnp.concatenate([x1, x2, x1, x2, x3, x1], axis=0).astype(BF16)


def distances(one_stack, other_stack):
    return jnp.dot(one_stack, other_stack, preferred_element_type=F32)


def weights(shifted):
    inverse = lax.rsqrt(shifted)
    return split2(inverse * inverse * inverse)


def fold(result):
    return result[:SUM_ROWS] + result[SUM_ROWS : 2 * SUM_ROWS] + result[2 * SUM_ROWS :]


def skewed(stages, skew):
    asked = []
    for q, (ask, _) in enumerate(stages):
        asked.append(ask())
        if q >= skew:
            stages[q - skew][1](asked[q - skew])
            asked[q - skew] = None
    for q in range(max(len(stages) - skew, 0), len(stages)):
        stages[q][1](asked[q])


def adder(totals, key):
    def add(value):
        totals[key] = totals[key] + value if key in totals else value

    return add


def wide_piece(operands, begin, first, end, add):
    def ask():
        _, y_turned, _, blocks = operands()
        return distances(y_turned[first:end], blocks[begin])

    def take(shifted):
        m_piece = operands()[2][first]
        high, low = weights(shifted)
        whole = (end - first) // 128 * 128
        parts = [high[:whole], low[:whole]] if whole else []
        parts += [high[whole:], low[whole:]] if whole < end - first else []
        stack = jnp.concatenate(parts, axis=0)
        add(jnp.dot(m_piece, stack, preferred_element_type=F32))

    return ask, take


def rest_piece(operands, begin, add):
    def ask():
        y_stack, _, _, blocks = operands()
        return distances(blocks[begin], y_stack)

    def take(shifted):
        stack = jnp.concatenate(weights(shifted), axis=1)
        m_whole = jnp.concatenate([operands()[2][-1]] * 2, axis=1)
        turned = (((1,), (1,)), ((), ()))
        add(lax.dot_general(m_whole, stack, turned, preferred_element_type=F32))

    return ask, take


def store_sums(slots, slot, j, x, result, offsets, sums):
    offsets.at[j][pl.ds(slot, 8, stride=slots), :] = x
    for h in range(0, SUM_ROWS, 8):
        sums.at[j][pl.ds(h * slots + slot, 8, stride=slots), :] = result[h : h + 8]


def mark(slot, target, hot):
    hot[pl.ds(slot, 1), :] = jnp.where(lane_iota(1) == target, 1.0, 0.0)


def combine(sz, slots, first, total, offsets, sums, speeds):
    live = lax.broadcasted_iota(jnp.int32, (8, 128), 0) + first < total
    for j in range(offsets.shape[0]):
        x = [offsets[j, pl.ds(i * slots + first, 8), :] for i in range(3)]
        s = [sums[j, pl.ds(k * slots + first, 8), :] for k in range(SUM_ROWS)]
        a, b, c = s[:3], [s[3:6], s[6:9], s[9:12]], s[12:15]
        norm = x[0] * x[0] + x[1] * x[1] + x[2] * x[2] + REGULARIZE
        along = x[0] * a[0] + x[1] * a[1] + x[2] * a[2] - s[15]
        for i in range(3):
            speed = norm * a[i] + c[i] + along * x[i]
            for k in range(3):
                speed = speed - x[k] * (2.0 * b[k][i] + b[i][k])
            speed = jnp.where(live, speed / sz.points, 0.0)
            speeds[i, pl.ds(first, 8), 128 * j : 128 * j + 128] = speed


def add_up(sz, slots, total, rows, offsets, sums, speeds, hot):
    def eight(q, carry):
        combine(sz, slots, pl.multiple_of(8 * q, 8), total, offsets, sums, speeds)
        return carry

    if slots <= 64 and offsets.shape[0] <= 2:
        for q in range(slots // 8):
            combine(sz, slots, 8 * q, total, offsets, sums, speeds)
    else:
        lax.fori_loop(0, lax.div(total + 7, 8), eight, 0)
    one_hot = hot[...].astype(BF16)
    result = []
    for i in range(3):
        first, second, third = split3(speeds[i])
        parts = [
            lax.dot_general(
                one_hot, part.astype(BF16), (((0,), (0,)), ((), ())), preferred_element_type=F32
            )
            for part in (first, second, third)
        ]
        result.append((parts[0] + parts[1] + parts[2])[:rows])
    return result


def several_tasks(sz, slots, picks, marks, main, rest, wide, step, skew, refs):
    source_rows, centres, targets, offsets, sums, hot = refs

    def task(slot, pick, target_mark):
        target, source = pick
        made, parts, points = [], {}, []

        def operands():
            if made:
                return made[0]
            y_stack, m_stack = source_operands(sz, source, source_rows)
            centre = centres[pl.ds(pl.multiple_of(8 * source, 8), 8), :]
            points.extend(
                load_target(j, target, slot, centre, targets, offsets)
                for j in range(targets.shape[0])
            )
            blocks = {}
            for begin in range(0, main, wide):
                stack = [stack for _, stack in points[begin // 128 : (begin + wide) // 128]]
                blocks[begin] = jnp.concatenate(stack, axis=1)
            if rest:
                blocks[main] = jnp.transpose(points[main // 128][1])[:rest]
            sides = {-1: m_stack.astype(BF16)}
            if main:
                for first, last in pieces(sz.points, step):
                    sides[first] = twice(m_stack[:, first : up(last, 128)], last - first)
            made.append((y_stack, jnp.transpose(y_stack), sides, blocks))
            return made[0]

        def finish():
            results = [fold(parts[begin]) for begin in range(0, main, wide)]
            if rest:
                spare = jnp.zeros((SUM_ROWS, 128 - rest), F32)
                results.append(jnp.concatenate([fold(parts[main]), spare], axis=1))
            result = jnp.concatenate(results, axis=1)
            for j in range(targets.shape[0]):
                cut = result[:, 128 * j : 128 * j + 128]
                store_sums(offsets.shape[1] // 8, slot, j, points[j][0], cut, offsets, sums)
            mark(slot, target_mark, hot)

        own = []
        for begin in range(0, main, wide):
            for first, last in pieces(sz.points, step):
                own.append(wide_piece(operands, begin, first, last, adder(parts, begin)))
        if rest:
            own.insert(len(own) // 2, rest_piece(operands, main, adder(parts, main)))
        ask, take = own[-1]

        def last_take(shifted):
            take(shifted)
            finish()

        own[-1] = (ask, last_take)
        return own, operands

    made = [task(slot, pick, m) for slot, pick, m in zip(slots, picks, marks)]
    for (own, _), (_, after) in zip(made, made[1:]):
        ask, take = own[0]

        def ask_and_prepare(ask=ask, after=after):
            shifted = ask()
            after()
            return shifted

        own[0] = (ask_and_prepare, take)
    skewed([stage for own, _ in made for stage in own], skew)


def tiles_of_chunk(sz, total, tasks, *refs):
    def several(q, carry):
        slots = [q * UNROLL + u for u in range(UNROLL)]
        picks = [(tasks[0, slot], tasks[1, slot]) for slot in slots]
        marks = [target for target, _ in picks]
        several_tasks(sz, slots, picks, marks, sz.main, sz.rest, 128, 256, 7, refs)
        return carry

    lax.fori_loop(0, lax.div(total + UNROLL - 1, UNROLL), several, 0)


def tiles_of_cells(sz, total, mine, *refs):
    main = 256 * (sz.points // 256)

    def several(q, carry):
        slots = [q * PAIR + u for u in range(PAIR)]
        marks = [mine[0, slot] for slot in slots]
        picks = [(jnp.maximum(mark, 0), mine[1, slot]) for mark, slot in zip(marks, slots)]
        several_tasks(sz, slots, picks, marks, main, sz.points - main, 256, 256, 4, refs)
        return carry

    lax.fori_loop(0, lax.div(total + PAIR - 1, PAIR), several, 0)


def packed(sz, blocks):
    rows = [b[:, : sz.main] for b in blocks] if sz.main else []
    lanes = lane_iota(8)
    for p in range(0, len(blocks), sz.per_pack):
        total = jnp.zeros((8, 128), F32)
        for q, block in enumerate(blocks[p : p + sz.per_pack]):
            rest = jnp.where(lanes < sz.rest, block[:, sz.main : sz.main + 128], 0.0)
            total = total + (pltpu.roll(rest, q * sz.rest, 1) if q else rest)
        rows.append(total)
    return rows


def store_packed(sz, out, blocks):
    first = 0
    count = len(blocks)
    values = packed(sz, blocks)
    if sz.main:
        for b in range(count):
            for m in range(sz.main // 128):
                out[pl.ds(first, 8), :] = values[b][:, 128 * m : 128 * m + 128]
                first += 8
        values = values[count:]
    for value in values:
        out[pl.ds(first, 8), :] = value
        first += 8


def place_packed(sz, lane, arrived, count, store_main, add_rest):
    first = 0
    if sz.main:
        for b in range(count):
            for m in range(sz.main // 128):
                store_main(b, m, arrived[pl.ds(first, 8), :])
                first += 8
    start = sz.rest * lane
    lanes = lane_iota(8)
    for b in range(count):
        pack, q = divmod(b, sz.per_pack)
        value = arrived[pl.ds(first + 8 * pack, 8), :]
        value = pltpu.roll(value, lax.rem(start - q * sz.rest + 128, 128), 1)
        for tile in range(sz.rest_tiles):
            inside = (lanes + 128 * tile >= start) & (lanes + 128 * tile < start + sz.rest)
            add_rest(b, tile, jnp.where(inside, value, 0.0))


def source_kernel(sz, *refs):
    inputs, (high_out, low_out, source_rows, centres), held, sems = (
        refs[:2],
        refs[2:6],
        refs[6:8],
        refs[8],
    )
    for copy in fetch(inputs, held, sems):
        copy.wait()
    positions, bend = held
    high_out[...], low_out[...] = split2(bend[...])
    value = jnp.concatenate([positions[i] for i in range(3)], axis=0)
    value = jnp.concatenate(
        [value, jnp.zeros((3 * sz.cells, sz.width - sz.points), F32)], axis=1
    )
    make_sources(sz, value, high_out[...], low_out[...], source_rows, centres, 0)


def first_kernel(sz, *refs):
    arrived, high, low, inputs = refs[0], refs[1], refs[2], refs[3:7]
    outputs, refs = refs[7:10], refs[10:]
    source_rows, centres, targets, offsets, sums, speeds, hot, moved, pool = refs[:9]
    send, positions, staged, lists, chunk_out, ghost_out, tasks, sems = refs[9:]
    me, lane = lax.axis_index("space"), lax.axis_index("lane")
    own_rows = source_rows.at[:, pl.ds(0, SOURCE_ROWS * sz.cells)]
    own_centres = centres.at[pl.ds(0, 8 * sz.cells)]
    copies = fetch(inputs, [send, positions, own_rows, own_centres], sems)
    for other in range(sz.lanes):
        row = ((me * sz.lanes + other) * sz.group) * 4 + 3
        value = pltpu.roll(arrived[pl.ds(row, 1), :], 128 - 3 * sz.rest, 1)
        staged[pl.ds(other, 1), :] = value.astype(jnp.int32)
    copies += fetch([staged], [lists], sems.at[pl.ds(4, 1)])
    pool[...] = jnp.zeros_like(pool)
    take_ghosts(sz, arrived, pool, up(sz.owners * sz.group, 8), 0)
    hot[...] = jnp.zeros_like(hot)
    speeds[...] = jnp.zeros_like(speeds)
    make_sources(sz, pool[...], high[...], low[...], source_rows, centres, sz.cells)
    for copy in copies[:2]:
        copy.wait()
    chunks = [
        [own_chunk(sz, lane, positions.at[i], pl.ds(g, 8)) for g in range(0, sz.cells, 8)]
        for i in range(3)
    ]
    make_targets(sz, [jnp.concatenate(blocks, axis=0) for blocks in chunks], targets)
    copies[4].wait()
    total = build_list(sz, lists, tasks)
    for copy in copies[2:4]:
        copy.wait()
    copies = fetch([tasks], outputs[2:], sems)
    tiles_of_chunk(sz, total, tasks, source_rows, centres, targets, offsets, sums, hot)
    velocity = add_up(sz, sz.slots, total, sz.cells, offsets, sums, speeds, hot)
    blocks = []
    for i in range(3):
        for g in range(0, sz.cells, 8):
            chunk = own_chunk(sz, lane, positions.at[i], pl.ds(g, 8))
            block = chunk + TIME_STEP * velocity[i][g : g + 8]
            moved[pl.ds(i * sz.rows + g, 8), :] = block
            blocks.append(block)
    store_packed(sz, chunk_out, blocks)
    copies += fetch([chunk_out], outputs[:1], sems.at[pl.ds(1, 1)])
    send_ghosts(sz, send, moved, ghost_out, jnp.zeros((1, 128), F32))
    copies += fetch([ghost_out], outputs[1:2], sems.at[pl.ds(2, 1)])
    for copy in copies:
        copy.wait()


def own_kernel(sz, *refs):
    (high, low), refs = refs[:2], refs[2:]
    others, refs = refs[: sz.lanes - 1], refs[sz.lanes - 1 :]
    inputs, (speed_out, share_out), refs = refs[:2], refs[2:4], refs[4:]
    source_rows, centres, targets, offsets, sums, speeds, hot, pool, mine = refs[:9]
    tasks, chunk, sems = refs[9:]
    copies = fetch(inputs, [tasks, chunk], sems)
    chunks = [chunk, *others]
    hot[...] = jnp.zeros_like(hot)
    speeds[...] = jnp.zeros_like(speeds)
    lane = lax.axis_index("lane")
    pool[...] = jnp.zeros_like(pool)
    copies[0].wait()
    total = own_list(sz, lane, tasks, mine, 0, sz.cells)
    copies[1].wait()
    per = sz.cells // 8
    for k in range(sz.lanes):
        other = lane ^ k

        def row_of(b):
            return (b // per) * sz.cells + 8 * (b % per)

        def store_main(b, m, value):
            cut = pl.ds(pl.multiple_of(other * sz.main + 128 * m, 128), 128)
            pool[pl.ds(row_of(b), 8), cut] = value

        def add_rest(b, tile, value):
            offset = sz.main * sz.lanes + 128 * tile
            cut = (pl.ds(row_of(b), 8), slice(offset, offset + 128))
            pool[cut] = pool[cut] + value

        place_packed(sz, other, chunks[k], 3 * per, store_main, add_rest)
    for i in range(3):
        share_out[i] = share_rows(sz, pool, i * sz.cells, lane)
    make_sources(sz, pool[...], high[...], low[...], source_rows, centres, 0)
    make_targets(sz, share_out, targets)
    tiles_of_cells(sz, total, mine, source_rows, centres, targets, offsets, sums, hot)
    velocity = add_up(sz, sz.own, total, up(sz.share, 8), offsets, sums, speeds, hot)
    for i in range(3):
        speed_out[i] = velocity[i]


def ghost_kernel(sz, *refs):
    arrived, high, low, speed_in, share, tasks_in = refs[:6]
    moved_out, velocity_out = refs[6:8]
    source_rows, centres, targets, offsets, sums, speeds, hot, pool, mine = refs[8:17]
    tasks, sems = refs[17:]
    copies = fetch([tasks_in], [tasks], sems)
    hot[...] = jnp.zeros_like(hot)
    speeds[...] = jnp.zeros_like(speeds)
    lane = lax.axis_index("lane")
    pool[...] = jnp.zeros_like(pool)
    ghosts = up(sz.owners * sz.group, 8)
    take_ghosts(sz, arrived, pool, ghosts, 0)
    make_sources(sz, pool[...], high[...], low[...], source_rows, centres, 0)
    make_targets(sz, share, targets)
    copies[0].wait()
    total = own_list(sz, lane, tasks, mine, sz.cells, sz.cells + sz.owners * sz.group)
    tiles_of_cells(sz, total, mine, source_rows, centres, targets, offsets, sums, hot)
    velocity = add_up(sz, sz.own, total, up(sz.share, 8), offsets, sums, speeds, hot)
    for i in range(3):
        speed = velocity[i] + speed_in[i]
        velocity_out[i] = speed[: sz.share, : sz.points]
        moved_out[i] = (share[i] + TIME_STEP * speed)[: sz.share, : sz.points]


def share_rows(sz, ref, base, lane):
    if sz.share % 8 == 0:
        return ref[pl.ds(pl.multiple_of(base + lane * sz.share, 8), sz.share), :]
    rows = [ref[pl.ds(base + lane * sz.share + c, 1), :] for c in range(sz.share)]
    rows.append(jnp.zeros((8 - sz.share, rows[0].shape[1]), F32))
    return jnp.concatenate(rows, axis=0)


def scratch(sz, cells, targets, tiles, slots):
    return [
        pltpu.VMEM((sz.tiles, SOURCE_ROWS * cells, 128), F32),
        pltpu.VMEM((8 * cells, 128), F32),
        pltpu.VMEM((tiles, 8 * targets, 128), F32),
        pltpu.VMEM((tiles, 8 * slots, 128), F32),
        pltpu.VMEM((tiles, SUM_ROWS * slots, 128), F32),
        pltpu.VMEM((3, slots, 128 * tiles), F32),
        pltpu.VMEM((slots, 128), F32),
    ]


def swap(value, axis, size, k):
    return lax.ppermute(value, axis, [(d, d ^ k) for d in range(size)])


def in_hbm(value):
    return pltpu.with_memory_space_constraint(value, pltpu.HBM)


def shards(positions, bend_op, send_list, task_target, task_source, task_count):
    owners, lanes = lax.axis_size("space"), lax.axis_size("lane")
    cells, points = positions.shape[0], positions.shape[2]
    sz = sizes(owners, lanes, cells, points, task_target.shape[1], send_list.shape[1])
    params = pltpu.CompilerParams(vmem_limit_bytes=min(6 * lanes, 40) << 20)
    shape = jax.ShapeDtypeStruct
    both = ("space", "lane")
    by_component = jnp.transpose(positions, (1, 0, 2))
    list_rows = up(lanes, 8)
    slot_shape = shape((4 * sz.group * owners * lanes, 128), F32)
    leaving, send = pl.pallas_call(
        functools.partial(pick_kernel, sz),
        out_shape=[slot_shape, shape(send_list.shape, jnp.int32)],
        in_specs=[HBM] * 5,
        out_specs=[VMEM, SMEM],
        scratch_shapes=[
            pltpu.SMEM(send_list.shape, jnp.int32),
            pltpu.VMEM(task_target.shape, jnp.int32),
            pltpu.VMEM(task_source.shape, jnp.int32),
            pltpu.SMEM(task_count.shape, jnp.int32),
            pltpu.VMEM(by_component.shape, F32),
            pltpu.VMEM((3 * sz.rows, sz.chunk_wide), F32),
            pltpu.SemaphoreType.DMA((5,)),
        ],
        compiler_params=pltpu.CompilerParams(vmem_limit_bytes=60 << 20),
        name="pick_cells",
    )(send_list, task_target, task_source, task_count, by_component)
    arrived = lax.all_to_all(leaving, both, split_axis=0, concat_axis=0, tiled=True)
    high, low, own_rows, own_centres = pl.pallas_call(
        functools.partial(source_kernel, sz),
        out_shape=[
            shape(bend_op.shape, BF16),
            shape(bend_op.shape, BF16),
            shape((sz.tiles, SOURCE_ROWS * cells, 128), F32),
            shape((8 * cells, 128), F32),
        ],
        in_specs=[HBM] * 2,
        out_specs=[VMEM] * 4,
        scratch_shapes=[
            pltpu.VMEM(by_component.shape, F32),
            pltpu.VMEM(bend_op.shape, F32),
            pltpu.SemaphoreType.DMA((2,)),
        ],
        compiler_params=params,
        cost_estimate=pl.CostEstimate(flops=10**9, bytes_accessed=10**7, transcendentals=0),
        name="first_sources",
    )(in_hbm(by_component), in_hbm(bend_op))
    chunk_shape = (pack_rows(sz, cells), 128)
    chunk, leaving, tasks = pl.pallas_call(
        functools.partial(first_kernel, sz),
        out_shape=[
            pltpu.HBM(chunk_shape, F32),
            pltpu.HBM(slot_shape.shape, F32),
            pltpu.HBM((3, sz.slots), jnp.int32),
        ],
        in_specs=[VMEM] * 3 + [HBM] * 2 + [ANY] * 2,
        out_specs=[HBM] * 3,
        scratch_shapes=scratch(sz, sz.pool, sz.rows, sz.chunk_tiles, sz.slots)
        + [
            pltpu.VMEM((3 * sz.rows, sz.chunk_wide), F32),
            pltpu.VMEM((3 * up(sz.owners * sz.group, 8), sz.width), F32),
            pltpu.SMEM(send_list.shape, jnp.int32),
            pltpu.VMEM(by_component.shape, F32),
            pltpu.VMEM((list_rows, 128), jnp.int32),
            pltpu.SMEM((list_rows, 128), jnp.int32),
            pltpu.VMEM(chunk_shape, F32),
            pltpu.VMEM(slot_shape.shape, F32),
            pltpu.SMEM((3, sz.slots), jnp.int32),
            pltpu.SemaphoreType.DMA((5,)),
        ],
        compiler_params=params,
        name="first_step",
    )(arrived, high, low, in_hbm(send), in_hbm(by_component), own_rows, own_centres)
    arrived = lax.all_to_all(leaving, both, split_axis=0, concat_axis=0, tiled=True)
    chunks = [swap(chunk, "lane", lanes, k) for k in range(1, lanes)]
    share = up(sz.share, 8)
    so_far = shape((3, share, sz.width), F32)
    speed, moved = pl.pallas_call(
        functools.partial(own_kernel, sz),
        out_shape=[so_far, so_far],
        in_specs=[VMEM] * (lanes + 1) + [HBM] * 2,
        out_specs=[VMEM] * 2,
        scratch_shapes=scratch(sz, cells, share, sz.tiles, sz.own)
        + [
            pltpu.VMEM((3 * cells, sz.width), F32),
            pltpu.SMEM((2, sz.own + 8), jnp.int32),
            pltpu.SMEM(tasks.shape, jnp.int32),
            pltpu.VMEM(chunk.shape, F32),
            pltpu.SemaphoreType.DMA((2,)),
        ],
        compiler_params=params,
        cost_estimate=pl.CostEstimate(flops=10**9, bytes_accessed=10**7, transcendentals=0),
        name="second_own",
    )(high, low, *chunks, in_hbm(tasks), in_hbm(chunk))
    result = shape((3, sz.share, points), F32)
    ghosts = up(owners * sz.group, 8)
    outputs = pl.pallas_call(
        functools.partial(ghost_kernel, sz),
        out_shape=[result, result],
        in_specs=[VMEM] * 5 + [HBM],
        out_specs=[VMEM] * 2,
        scratch_shapes=scratch(sz, ghosts, share, sz.tiles, sz.own)
        + [
            pltpu.VMEM((3 * ghosts, sz.width), F32),
            pltpu.SMEM((2, sz.own + 8), jnp.int32),
            pltpu.SMEM(tasks.shape, jnp.int32),
            pltpu.SemaphoreType.DMA((1,)),
        ],
        compiler_params=params,
        name="second_ghosts",
    )(arrived, high, low, speed, moved, in_hbm(tasks))
    return tuple(jnp.transpose(output, (1, 0, 2)) for output in outputs)


def solution(mesh):
    in_specs = (
        P("space", None, None),
        P(),
        P("space", None),
        P(("space", "lane"), None),
        P(("space", "lane"), None),
        P(("space", "lane")),
    )
    out_specs = (P(("space", "lane"), None, None), P(("space", "lane"), None, None))
    return jax.shard_map(shards, mesh=mesh, in_specs=in_specs, out_specs=out_specs, check_vma=False)
```

profile of v0, /device:TPU:0, one launch (start us, length us, event | category | flops | bytes accessed | tf_op | source)
XLA Modules:
  0.0 45.9 jit_solution(2145588574019887597)
XLA Ops:
  1.3 1.8 %pick_cells.1 = (f32[128,128]{1,0:T(8,128)}, s32[1,8]{1,0:T(1,128)}) custom-call(s32[1,8]{1,0:T(1,128)} %refs_0_.1, s32[1,12]{1,0:T(1,128)} %refs_1_.2, s32[1,12]{1,0:T(1,128)} %refs_2_.1, s32[1]{0:T(128)S(6)} %copy.8.refs_3_, f32[3,32,544]{2,1,0:T(8,128)} %bitcast.9), custom_call_target="tpu_custom_call" | custom-call | tf_op jit(solution)/shard_map/pick_cells/pallas_call | solution.py:727
  3.1 7.3 %all-to-all-start = ((f32[32,4,128]{2,1,0:T(4,128)}), f32[32,4,128]{2,1,0:T(4,128)S(1)}, u32[]{:S(2)}, u32[]{:S(2)}) async-start(f32[32,4,128]{2,1,0:T(4,128)} %bitcast.13), calls=%async_computation | async-start | bytes 131072 | tf_op jit(solution)/shard_map/all_to_all | solution.py:744
  10.4 2.4 %first_sources.1 = (bf16[544,544]{1,0:T(8,128)(2,1)S(1)}, bf16[544,544]{1,0:T(8,128)(2,1)S(1)}, f32[5,768,128]{2,1,0:T(8,128)S(1)}, f32[256,128]{1,0:T(8,128)S(1)}) custom-call(f32[3,32,544]{2,1,0:T(8,128)} %bitcast.10, f32[544,544]{1,0:T(8,128)} %refs_1_.3), custom_call_target="tpu_custom_call" | custom-call | flops 1000000000 | bytes 10000000 | tf_op jit(solution)/shard_map/first_sources/pallas_call | solution.py:745
  12.8 5.1 %all-to-all-done = f32[32,4,128]{2,1,0:T(4,128)S(1)} async-done(((f32[32,4,128]{2,1,0:T(4,128)}), f32[32,4,128]{2,1,0:T(4,128)S(1)}, u32[]{:S(2)}, u32[]{:S(2)}) %all-to-all-start) | async-done | bytes 65568 | tf_op jit(solution)/shard_map/all_to_all | solution.py:744
  17.9 8.7 %first_step.1 = (f32[104,128]{1,0:T(8,128)}, f32[128,128]{1,0:T(8,128)}, s32[3,64]{1,0:T(4,128)}) custom-call(f32[128,128]{1,0:T(8,128)S(1)} %bitcast.7, bf16[544,544]{1,0:T(8,128)(2,1)S(1)} %get-tuple-element.16.refs_1_.refs_0_, bf16[544,544]{1,0:T(8,128)(2,1)S(1)} %get-tuple-element.17.refs_2_.refs_1_, s32[1,8]{1,0:T(1,128)} %get-tuple-element.18.refs_3_, ...), custom_call_target="tpu_custom_call" | custom-call | tf_op jit(solution)/shard_map/first_step/pallas_call | solution.py:765
  26.7 0.9 %collective-permute-start.2 = (f32[104,128]{1,0:T(8,128)}, f32[104,128]{1,0:T(8,128)S(1)}, u32[]{:S(2)}, u32[]{:S(2)}) collective-permute-start(f32[104,128]{1,0:T(8,128)} %get-tuple-element.22.refs_6_), channel_id=1, source_target_pairs={{0,3},{1,2},{2,1},{3,0},{4,7},{5,6},{6,5},{7,4},{8,11},{9,10},{10,... | collective-permute-start | bytes 159752 | tf_op jit(solution)/shard_map/ppermute | solution.py:710
  27.5 0.9 %collective-permute-start.1 = (f32[104,128]{1,0:T(8,128)}, f32[104,128]{1,0:T(8,128)S(1)}, u32[]{:S(2)}, u32[]{:S(2)}) collective-permute-start(f32[104,128]{1,0:T(8,128)} %get-tuple-element.22.refs_6_), channel_id=1, source_target_pairs={{0,2},{1,3},{2,0},{3,1},{4,6},{5,7},{6,4},{7,5},{8,10},{9,11},{10,... | collective-permute-start | bytes 159752 | tf_op jit(solution)/shard_map/ppermute | solution.py:710
  28.4 2.7 %collective-permute-start = (f32[104,128]{1,0:T(8,128)}, f32[104,128]{1,0:T(8,128)S(1)}, u32[]{:S(2)}, u32[]{:S(2)}) collective-permute-start(f32[104,128]{1,0:T(8,128)} %get-tuple-element.22.refs_6_), channel_id=1, source_target_pairs={{0,1},{1,0},{2,3},{3,2},{4,5},{5,4},{6,7},{7,6},{8,9},{9,8},{10,11... | collective-permute-start | bytes 159752 | tf_op jit(solution)/shard_map/ppermute | solution.py:710
  31.1 2.6 %all-to-all-start.1 = ((f32[32,4,128]{2,1,0:T(4,128)}), f32[32,4,128]{2,1,0:T(4,128)S(1)}, u32[]{:S(2)}, u32[]{:S(2)}) async-start(f32[32,4,128]{2,1,0:T(4,128)} %bitcast.12), calls=%async_computation.1 | async-start | bytes 131072 | tf_op jit(solution)/shard_map/all_to_all | solution.py:790
  33.7 0.0 collective-permute-done.2.refs_4_
  33.7 0.5 %collective-permute-done.1.refs_3_ = f32[104,128]{1,0:T(8,128)S(1)} collective-permute-done((f32[104,128]{1,0:T(8,128)}, f32[104,128]{1,0:T(8,128)S(1)}, u32[]{:S(2)}, u32[]{:S(2)}) %collective-permute-start.1) | collective-permute-done | bytes 53280 | tf_op jit(solution)/shard_map/ppermute | solution.py:710
  34.2 0.0 collective-permute-done.refs_2_
  34.2 6.2 %second_own.1 = (f32[3,8,640]{2,1,0:T(8,128)S(1)}, f32[3,8,640]{2,1,0:T(8,128)S(1)}) custom-call(bf16[544,544]{1,0:T(8,128)(2,1)S(1)} %get-tuple-element.16.refs_1_.refs_0_, bf16[544,544]{1,0:T(8,128)(2,1)S(1)} %get-tuple-element.17.refs_2_.refs_1_, f32[104,128]{1,0:T(8,128)S(1)} %collective-permute-done.refs_2_, ...), custom_call_target="tpu_custom_call" | custom-call | flops 1000000000 | bytes 10000000 | tf_op jit(solution)/shard_map/second_own/pallas_call | solution.py:794
  40.3 0.8 %all-to-all-done.1 = f32[32,4,128]{2,1,0:T(4,128)S(1)} async-done(((f32[32,4,128]{2,1,0:T(4,128)}), f32[32,4,128]{2,1,0:T(4,128)S(1)}, u32[]{:S(2)}, u32[]{:S(2)}) %all-to-all-start.1) | async-done | bytes 65568 | tf_op jit(solution)/shard_map/all_to_all | solution.py:790
  41.2 4.8 %second_ghosts.1 = (f32[3,8,544]{2,1,0:T(8,128)}, f32[3,8,544]{2,1,0:T(8,128)}) custom-call(f32[128,128]{1,0:T(8,128)S(1)} %bitcast.8, bf16[544,544]{1,0:T(8,128)(2,1)S(1)} %get-tuple-element.16.refs_1_.refs_0_, bf16[544,544]{1,0:T(8,128)(2,1)S(1)} %get-tuple-element.17.refs_2_.refs_1_, f32[3,8,640]{2,1,0:T(8,128)S(1)} %get-tuple-element.24.refs_3_, ...), custom_call_target="tpu_custom_call" | custom-call | tf_op jit(solution)/shard_map/second_ghosts/pallas_call | solution.py:813
Async XLA Ops:
  3.1 14.8 %all-to-all-start = ((f32[32,4,128]{2,1,0:T(4,128)}), f32[32,4,128]{2,1,0:T(4,128)S(1)}, u32[]{:S(2)}, u32[]{:S(2)}) async-start(f32[32,4,128]{2,1,0:T(4,128)} %bitcast.13), calls=%async_computation | async-start | bytes 131072 | tf_op jit(solution)/shard_map/all_to_all | solution.py:744
  26.7 7.0 %collective-permute-start.2 = (f32[104,128]{1,0:T(8,128)}, f32[104,128]{1,0:T(8,128)S(1)}, u32[]{:S(2)}, u32[]{:S(2)}) collective-permute-start(f32[104,128]{1,0:T(8,128)} %get-tuple-element.22.refs_6_), channel_id=1, source_target_pairs={{0,3},{1,2},{2,1},{3,0},{4,7},{5,6},{6,5},{7,4},{8,11},{9,10},{10,... | collective-permute-start | bytes 159752 | tf_op jit(solution)/shard_map/ppermute | solution.py:710
  27.5 6.6 %collective-permute-start.1 = (f32[104,128]{1,0:T(8,128)}, f32[104,128]{1,0:T(8,128)S(1)}, u32[]{:S(2)}, u32[]{:S(2)}) collective-permute-start(f32[104,128]{1,0:T(8,128)} %get-tuple-element.22.refs_6_), channel_id=1, source_target_pairs={{0,2},{1,3},{2,0},{3,1},{4,6},{5,7},{6,4},{7,5},{8,10},{9,11},{10,... | collective-permute-start | bytes 159752 | tf_op jit(solution)/shard_map/ppermute | solution.py:710
  28.4 5.7 %collective-permute-start = (f32[104,128]{1,0:T(8,128)}, f32[104,128]{1,0:T(8,128)S(1)}, u32[]{:S(2)}, u32[]{:S(2)}) collective-permute-start(f32[104,128]{1,0:T(8,128)} %get-tuple-element.22.refs_6_), channel_id=1, source_target_pairs={{0,1},{1,0},{2,3},{3,2},{4,5},{5,4},{6,7},{7,6},{8,9},{9,8},{10,11... | collective-permute-start | bytes 159752 | tf_op jit(solution)/shard_map/ppermute | solution.py:710
  31.1 10.1 %all-to-all-start.1 = ((f32[32,4,128]{2,1,0:T(4,128)}), f32[32,4,128]{2,1,0:T(4,128)S(1)}, u32[]{:S(2)}, u32[]{:S(2)}) async-start(f32[32,4,128]{2,1,0:T(4,128)} %bitcast.12), calls=%async_computation.1 | async-start | bytes 131072 | tf_op jit(solution)/shard_map/all_to_all | solution.py:790
where the time goes:
time: 46.3 us; the launch traced here: 45.9 us
  Pallas kernels  23.9 us (52%)
  starting transfers between devices  14.3 us (31%)
  waiting for transfers between devices  6.43 us (14%)
  between operations  1.34 us (3%)
    all_to_all x2, starting transfers between devices, shards(): lax.all_to_all(leaving, both, split_axis=0, concat_axis=0, tiled=True)  9.85 us
    pallas_call x1, Pallas kernels, shards(): pl.pallas_call(functools.partial(first_kernel, sz), out_shape=[pltpu.HBM(...  8.71 us
    pallas_call x1, Pallas kernels, shards(): pl.pallas_call(functools.partial(own_kernel, sz), out_shape=[so_far, so_f...  6.15 us
    all_to_all x2, waiting for transfers between devices, shards(): lax.all_to_all(leaving, both, split_axis=0, concat_axis=0, tiled=True)  5.95 us
    pallas_call x1, Pallas kernels, shards(): pl.pallas_call(functools.partial(ghost_kernel, sz), out_shape=[result, re...  4.78 us
    ppermute x3, starting transfers between devices, swap(): return lax.ppermute(value, axis, [(d, d ^ k) for d in range(size)])  4.45 us
    pallas_call x1, Pallas kernels, shards(): pl.pallas_call(functools.partial(source_kernel, sz), out_shape=[shape(ben...  2.38 us
    pallas_call x1, Pallas kernels, shards(): pl.pallas_call(functools.partial(pick_kernel, sz), out_shape=[slot_shape,...  1.85 us
  transfers between devices with their start and end apart: 5, of which 3 were waited for; matrix products, arithmetic and copies ran while one was open for 0% of the time, Pallas kernels for 19%

commit v1 on v0

--- a/solution.py
+++ b/solution.py
@@ -490,7 +490,7 @@
         slots = [q * UNROLL + u for u in range(UNROLL)]
         picks = [(tasks[0, slot], tasks[1, slot]) for slot in slots]
         marks = [target for target, _ in picks]
-        several_tasks(sz, slots, picks, marks, sz.main, sz.rest, 128, 256, 7, refs)
+        several_tasks(sz, slots, picks, marks, sz.main, sz.rest, 128, 256, 9, refs)
         return carry
 
     lax.fori_loop(0, lax.div(total + UNROLL - 1, UNROLL), several, 0)
@@ -503,7 +503,7 @@
         slots = [q * PAIR + u for u in range(PAIR)]
         marks = [mine[0, slot] for slot in slots]
         picks = [(jnp.maximum(mark, 0), mine[1, slot]) for mark, slot in zip(marks, slots)]
-        several_tasks(sz, slots, picks, marks, main, sz.points - main, 256, 256, 4, refs)
+        several_tasks(sz, slots, picks, marks, main, sz.points - main, 256, 256, 3, refs)
         return carry
 
     lax.fori_loop(0, lax.div(total + PAIR - 1, PAIR), several, 0)

time: 46.3 us -> 46 us (level)
  Pallas kernels: 23.9 us -> 22.1 us
  waiting for transfers between devices: 6.43 us -> 7.9 us
    all_to_all x2, waiting for transfers between devices: 5.95 us -> 7.41 us  [shards(): lax.all_to_all(leaving, both, split_axis=0, concat_axis=0, tiled=True)]
    pallas_call x1, Pallas kernels: 6.15 us -> 4.68 us  [shards(): pl.pallas_call(functools.partial(own_kernel, sz), out_shape=[so_far, so_f...]
  transfers between devices with their start and end apart: 5 -> 5, of which waited for: 3 -> 3; matrix products, arithmetic and copies ran while one was open for 0% -> 0% of each run, Pallas kernels for 19% -> 16%
where the time goes in v1:
time: 46 us; the launch traced here: 45.6 us
  Pallas kernels  22.1 us (48%)
  starting transfers between devices  14.3 us (31%)
  waiting for transfers between devices  7.9 us (17%)
  between operations  1.34 us (3%)
    all_to_all x2, starting transfers between devices, shards(): lax.all_to_all(leaving, both, split_axis=0, concat_axis=0, tiled=True)  9.85 us
    pallas_call x1, Pallas kernels, shards(): pl.pallas_call(functools.partial(first_kernel, sz), out_shape=[pltpu.HBM(...  8.71 us
    all_to_all x2, waiting for transfers between devices, shards(): lax.all_to_all(leaving, both, split_axis=0, concat_axis=0, tiled=True)  7.41 us
    pallas_call x1, Pallas kernels, shards(): pl.pallas_call(functools.partial(own_kernel, sz), out_shape=[so_far, so_f...  4.68 us
    pallas_call x1, Pallas kernels, shards(): pl.pallas_call(functools.partial(ghost_kernel, sz), out_shape=[result, re...  4.47 us
    ppermute x3, starting transfers between devices, swap(): return lax.ppermute(value, axis, [(d, d ^ k) for d in range(size)])  4.45 us
    pallas_call x1, Pallas kernels, shards(): pl.pallas_call(functools.partial(source_kernel, sz), out_shape=[shape(ben...  2.38 us
    pallas_call x1, Pallas kernels, shards(): pl.pallas_call(functools.partial(pick_kernel, sz), out_shape=[slot_shape,...  1.85 us
  transfers between devices with their start and end apart: 5, of which 3 were waited for; matrix products, arithmetic and copies ran while one was open for 0% of the time, Pallas kernels for 16%

profile of v1, /device:TPU:0, one launch (start us, length us, event | category | flops | bytes accessed | tf_op | source)
XLA Modules:
  0.0 45.6 jit_solution(5369287876033602513)
XLA Ops:
  1.3 1.8 %pick_cells.1 = (f32[128,128]{1,0:T(8,128)}, s32[1,8]{1,0:T(1,128)}) custom-call(s32[1,8]{1,0:T(1,128)} %refs_0_.1, s32[1,12]{1,0:T(1,128)} %refs_1_.2, s32[1,12]{1,0:T(1,128)} %refs_2_.1, s32[1]{0:T(128)S(6)} %copy.8.refs_3_, f32[3,32,544]{2,1,0:T(8,128)} %bitcast.9), custom_call_target="tpu_custom_call" | custom-call | tf_op jit(solution)/shard_map/pick_cells/pallas_call | solution.py:727
  3.1 7.3 %all-to-all-start = ((f32[32,4,128]{2,1,0:T(4,128)}), f32[32,4,128]{2,1,0:T(4,128)S(1)}, u32[]{:S(2)}, u32[]{:S(2)}) async-start(f32[32,4,128]{2,1,0:T(4,128)} %bitcast.13), calls=%async_computation | async-start | bytes 131072 | tf_op jit(solution)/shard_map/all_to_all | solution.py:744
  10.4 2.4 %first_sources.1 = (bf16[544,544]{1,0:T(8,128)(2,1)S(1)}, bf16[544,544]{1,0:T(8,128)(2,1)S(1)}, f32[5,768,128]{2,1,0:T(8,128)S(1)}, f32[256,128]{1,0:T(8,128)S(1)}) custom-call(f32[3,32,544]{2,1,0:T(8,128)} %bitcast.10, f32[544,544]{1,0:T(8,128)} %refs_1_.3), custom_call_target="tpu_custom_call" | custom-call | flops 1000000000 | bytes 10000000 | tf_op jit(solution)/shard_map/first_sources/pallas_call | solution.py:745
  12.8 5.1 %all-to-all-done = f32[32,4,128]{2,1,0:T(4,128)S(1)} async-done(((f32[32,4,128]{2,1,0:T(4,128)}), f32[32,4,128]{2,1,0:T(4,128)S(1)}, u32[]{:S(2)}, u32[]{:S(2)}) %all-to-all-start) | async-done | bytes 65568 | tf_op jit(solution)/shard_map/all_to_all | solution.py:744
  17.9 8.7 %first_step.1 = (f32[104,128]{1,0:T(8,128)}, f32[128,128]{1,0:T(8,128)}, s32[3,64]{1,0:T(4,128)}) custom-call(f32[128,128]{1,0:T(8,128)S(1)} %bitcast.7, bf16[544,544]{1,0:T(8,128)(2,1)S(1)} %get-tuple-element.16.refs_1_.refs_0_, bf16[544,544]{1,0:T(8,128)(2,1)S(1)} %get-tuple-element.17.refs_2_.refs_1_, s32[1,8]{1,0:T(1,128)} %get-tuple-element.18.refs_3_, ...), custom_call_target="tpu_custom_call" | custom-call | tf_op jit(solution)/shard_map/first_step/pallas_call | solution.py:765
  26.7 0.9 %collective-permute-start.2 = (f32[104,128]{1,0:T(8,128)}, f32[104,128]{1,0:T(8,128)S(1)}, u32[]{:S(2)}, u32[]{:S(2)}) collective-permute-start(f32[104,128]{1,0:T(8,128)} %get-tuple-element.22.refs_6_), channel_id=1, source_target_pairs={{0,3},{1,2},{2,1},{3,0},{4,7},{5,6},{6,5},{7,4},{8,11},{9,10},{10,... | collective-permute-start | bytes 159752 | tf_op jit(solution)/shard_map/ppermute | solution.py:710
  27.5 0.9 %collective-permute-start.1 = (f32[104,128]{1,0:T(8,128)}, f32[104,128]{1,0:T(8,128)S(1)}, u32[]{:S(2)}, u32[]{:S(2)}) collective-permute-start(f32[104,128]{1,0:T(8,128)} %get-tuple-element.22.refs_6_), channel_id=1, source_target_pairs={{0,2},{1,3},{2,0},{3,1},{4,6},{5,7},{6,4},{7,5},{8,10},{9,11},{10,... | collective-permute-start | bytes 159752 | tf_op jit(solution)/shard_map/ppermute | solution.py:710
  28.4 2.7 %collective-permute-start = (f32[104,128]{1,0:T(8,128)}, f32[104,128]{1,0:T(8,128)S(1)}, u32[]{:S(2)}, u32[]{:S(2)}) collective-permute-start(f32[104,128]{1,0:T(8,128)} %get-tuple-element.22.refs_6_), channel_id=1, source_target_pairs={{0,1},{1,0},{2,3},{3,2},{4,5},{5,4},{6,7},{7,6},{8,9},{9,8},{10,11... | collective-permute-start | bytes 159752 | tf_op jit(solution)/shard_map/ppermute | solution.py:710
  31.1 2.6 %all-to-all-start.1 = ((f32[32,4,128]{2,1,0:T(4,128)}), f32[32,4,128]{2,1,0:T(4,128)S(1)}, u32[]{:S(2)}, u32[]{:S(2)}) async-start(f32[32,4,128]{2,1,0:T(4,128)} %bitcast.12), calls=%async_computation.1 | async-start | bytes 131072 | tf_op jit(solution)/shard_map/all_to_all | solution.py:790
  33.7 0.0 collective-permute-done.2.refs_4_
  33.7 0.5 %collective-permute-done.1.refs_3_ = f32[104,128]{1,0:T(8,128)S(1)} collective-permute-done((f32[104,128]{1,0:T(8,128)}, f32[104,128]{1,0:T(8,128)S(1)}, u32[]{:S(2)}, u32[]{:S(2)}) %collective-permute-start.1) | collective-permute-done | bytes 53280 | tf_op jit(solution)/shard_map/ppermute | solution.py:710
  34.2 0.0 collective-permute-done.refs_2_
  34.2 4.7 %second_own.1 = (f32[3,8,640]{2,1,0:T(8,128)S(1)}, f32[3,8,640]{2,1,0:T(8,128)S(1)}) custom-call(bf16[544,544]{1,0:T(8,128)(2,1)S(1)} %get-tuple-element.16.refs_1_.refs_0_, bf16[544,544]{1,0:T(8,128)(2,1)S(1)} %get-tuple-element.17.refs_2_.refs_1_, f32[104,128]{1,0:T(8,128)S(1)} %collective-permute-done.refs_2_, ...), custom_call_target="tpu_custom_call" | custom-call | flops 1000000000 | bytes 10000000 | tf_op jit(solution)/shard_map/second_own/pallas_call | solution.py:794
  38.9 2.3 %all-to-all-done.1 = f32[32,4,128]{2,1,0:T(4,128)S(1)} async-done(((f32[32,4,128]{2,1,0:T(4,128)}), f32[32,4,128]{2,1,0:T(4,128)S(1)}, u32[]{:S(2)}, u32[]{:S(2)}) %all-to-all-start.1) | async-done | bytes 65568 | tf_op jit(solution)/shard_map/all_to_all | solution.py:790
  41.2 4.5 %second_ghosts.1 = (f32[3,8,544]{2,1,0:T(8,128)}, f32[3,8,544]{2,1,0:T(8,128)}) custom-call(f32[128,128]{1,0:T(8,128)S(1)} %bitcast.8, bf16[544,544]{1,0:T(8,128)(2,1)S(1)} %get-tuple-element.16.refs_1_.refs_0_, bf16[544,544]{1,0:T(8,128)(2,1)S(1)} %get-tuple-element.17.refs_2_.refs_1_, f32[3,8,640]{2,1,0:T(8,128)S(1)} %get-tuple-element.24.refs_3_, ...), custom_call_target="tpu_custom_call" | custom-call | tf_op jit(solution)/shard_map/second_ghosts/pallas_call | solution.py:813
Async XLA Ops:
  3.1 14.8 %all-to-all-start = ((f32[32,4,128]{2,1,0:T(4,128)}), f32[32,4,128]{2,1,0:T(4,128)S(1)}, u32[]{:S(2)}, u32[]{:S(2)}) async-start(f32[32,4,128]{2,1,0:T(4,128)} %bitcast.13), calls=%async_computation | async-start | bytes 131072 | tf_op jit(solution)/shard_map/all_to_all | solution.py:744
  26.7 7.0 %collective-permute-start.2 = (f32[104,128]{1,0:T(8,128)}, f32[104,128]{1,0:T(8,128)S(1)}, u32[]{:S(2)}, u32[]{:S(2)}) collective-permute-start(f32[104,128]{1,0:T(8,128)} %get-tuple-element.22.refs_6_), channel_id=1, source_target_pairs={{0,3},{1,2},{2,1},{3,0},{4,7},{5,6},{6,5},{7,4},{8,11},{9,10},{10,... | collective-permute-start | bytes 159752 | tf_op jit(solution)/shard_map/ppermute | solution.py:710
  27.5 6.6 %collective-permute-start.1 = (f32[104,128]{1,0:T(8,128)}, f32[104,128]{1,0:T(8,128)S(1)}, u32[]{:S(2)}, u32[]{:S(2)}) collective-permute-start(f32[104,128]{1,0:T(8,128)} %get-tuple-element.22.refs_6_), channel_id=1, source_target_pairs={{0,2},{1,3},{2,0},{3,1},{4,6},{5,7},{6,4},{7,5},{8,10},{9,11},{10,... | collective-permute-start | bytes 159752 | tf_op jit(solution)/shard_map/ppermute | solution.py:710
  28.4 5.7 %collective-permute-start = (f32[104,128]{1,0:T(8,128)}, f32[104,128]{1,0:T(8,128)S(1)}, u32[]{:S(2)}, u32[]{:S(2)}) collective-permute-start(f32[104,128]{1,0:T(8,128)} %get-tuple-element.22.refs_6_), channel_id=1, source_target_pairs={{0,1},{1,0},{2,3},{3,2},{4,5},{5,4},{6,7},{7,6},{8,9},{9,8},{10,11... | collective-permute-start | bytes 159752 | tf_op jit(solution)/shard_map/ppermute | solution.py:710
  31.1 10.1 %all-to-all-start.1 = ((f32[32,4,128]{2,1,0:T(4,128)}), f32[32,4,128]{2,1,0:T(4,128)S(1)}, u32[]{:S(2)}, u32[]{:S(2)}) async-start(f32[32,4,128]{2,1,0:T(4,128)} %bitcast.12), calls=%async_computation.1 | async-start | bytes 131072 | tf_op jit(solution)/shard_map/all_to_all | solution.py:790

commit v2 on v1

--- a/solution.py
+++ b/solution.py
@@ -20,7 +20,6 @@
 VMEM = pl.BlockSpec(memory_space=pltpu.VMEM)
 SMEM = pl.BlockSpec(memory_space=pltpu.SMEM)
 HBM = pl.BlockSpec(memory_space=pltpu.HBM)
-ANY = pl.BlockSpec(memory_space=pl.ANY)
 
 
 def up(value, step):
@@ -268,11 +267,21 @@
                 targets.at[j][pl.ds(64 * g + i, 8, stride=8), :] = block[:, cut]
 
 
+def rows_of(refs, cell, rows, tile=None):
+    def load(ref, at):
+        place = pl.ds(pl.multiple_of(rows * at, 8), rows)
+        return ref[place, :] if tile is None else ref[tile, place, :]
+
+    if not isinstance(refs, tuple):
+        return load(refs, cell)
+    first, second = refs
+    count = first.shape[-2] // rows
+    own = load(first, jnp.minimum(cell, count - 1))
+    return jnp.where(cell < count, own, load(second, jnp.maximum(cell - count, 0)))
+
+
 def source_operands(sz, source, source_rows):
-    held = [
-        source_rows[j, pl.ds(pl.multiple_of(SOURCE_ROWS * source, 8), SOURCE_ROWS), :]
-        for j in range(sz.tiles)
-    ]
+    held = [rows_of(source_rows, source, SOURCE_ROWS, j) for j in range(sz.tiles)]
     held = jnp.concatenate(held, axis=1)
     y1, y2, y3 = split3(held[:8])
     y_stack = jnp.concatenate([y1, y1, y2, y2, y1, y3], axis=0).astype(BF16)
@@ -428,7 +437,7 @@
             if made:
                 return made[0]
             y_stack, m_stack = source_operands(sz, source, source_rows)
-            centre = centres[pl.ds(pl.multiple_of(8 * source, 8), 8), :]
+            centre = rows_of(centres, source, 8)
             points.extend(
                 load_target(j, target, slot, centre, targets, offsets)
                 for j in range(targets.shape[0])
@@ -573,24 +582,22 @@
 
 
 def first_kernel(sz, *refs):
-    arrived, high, low, inputs = refs[0], refs[1], refs[2], refs[3:7]
-    outputs, refs = refs[7:10], refs[10:]
+    arrived, high, low, own_rows, own_centres = refs[:5]
+    inputs, outputs, refs = refs[5:7], refs[7:10], refs[10:]
     source_rows, centres, targets, offsets, sums, speeds, hot, moved, pool = refs[:9]
     send, positions, staged, lists, chunk_out, ghost_out, tasks, sems = refs[9:]
     me, lane = lax.axis_index("space"), lax.axis_index("lane")
-    own_rows = source_rows.at[:, pl.ds(0, SOURCE_ROWS * sz.cells)]
-    own_centres = centres.at[pl.ds(0, 8 * sz.cells)]
-    copies = fetch(inputs, [send, positions, own_rows, own_centres], sems)
+    copies = fetch(inputs, [send, positions], sems)
     for other in range(sz.lanes):
         row = ((me * sz.lanes + other) * sz.group) * 4 + 3
         value = pltpu.roll(arrived[pl.ds(row, 1), :], 128 - 3 * sz.rest, 1)
         staged[pl.ds(other, 1), :] = value.astype(jnp.int32)
-    copies += fetch([staged], [lists], sems.at[pl.ds(4, 1)])
+    copies += fetch([staged], [lists], sems.at[pl.ds(2, 1)])
     pool[...] = jnp.zeros_like(pool)
     take_ghosts(sz, arrived, pool, up(sz.owners * sz.group, 8), 0)
     hot[...] = jnp.zeros_like(hot)
     speeds[...] = jnp.zeros_like(speeds)
-    make_sources(sz, pool[...], high[...], low[...], source_rows, centres, sz.cells)
+    make_sources(sz, pool[...], high[...], low[...], source_rows, centres, 0)
     for copy in copies[:2]:
         copy.wait()
     chunks = [
@@ -598,12 +605,11 @@
         for i in range(3)
     ]
     make_targets(sz, [jnp.concatenate(blocks, axis=0) for blocks in chunks], targets)
-    copies[4].wait()
+    copies[2].wait()
     total = build_list(sz, lists, tasks)
-    for copy in copies[2:4]:
-        copy.wait()
     copies = fetch([tasks], outputs[2:], sems)
-    tiles_of_chunk(sz, total, tasks, source_rows, centres, targets, offsets, sums, hot)
+    rows, middles = (own_rows, source_rows), (own_centres, centres)
+    tiles_of_chunk(sz, total, tasks, rows, middles, targets, offsets, sums, hot)
     velocity = add_up(sz, sz.slots, total, sz.cells, offsets, sums, speeds, hot)
     blocks = []
     for i in range(3):
@@ -769,9 +775,9 @@
             pltpu.HBM(slot_shape.shape, F32),
             pltpu.HBM((3, sz.slots), jnp.int32),
         ],
-        in_specs=[VMEM] * 3 + [HBM] * 2 + [ANY] * 2,
+        in_specs=[VMEM] * 5 + [HBM] * 2,
         out_specs=[HBM] * 3,
-        scratch_shapes=scratch(sz, sz.pool, sz.rows, sz.chunk_tiles, sz.slots)
+        scratch_shapes=scratch(sz, sz.pool - cells, sz.rows, sz.chunk_tiles, sz.slots)
         + [
             pltpu.VMEM((3 * sz.rows, sz.chunk_wide), F32),
             pltpu.VMEM((3 * up(sz.owners * sz.group, 8), sz.width), F32),
@@ -782,11 +788,11 @@
             pltpu.VMEM(chunk_shape, F32),
             pltpu.VMEM(slot_shape.shape, F32),
             pltpu.SMEM((3, sz.slots), jnp.int32),
-            pltpu.SemaphoreType.DMA((5,)),
+            pltpu.SemaphoreType.DMA((3,)),
         ],
         compiler_params=params,
         name="first_step",
-    )(arrived, high, low, in_hbm(send), in_hbm(by_component), own_rows, own_centres)
+    )(arrived, high, low, own_rows, own_centres, in_hbm(send), in_hbm(by_component))
     arrived = lax.all_to_all(leaving, both, split_axis=0, concat_axis=0, tiled=True)
     chunks = [swap(chunk, "lane", lanes, k) for k in range(1, lanes)]
     share = up(sz.share, 8)

time: 46 us -> 46 us (level)
  the two profiles are of different devices: /device:TPU:0 before, /device:TPU:25 now
where the time goes in v2:
time: 46 us; the launch traced here: 45.9 us
  Pallas kernels  26.2 us (57%)
  starting transfers between devices  16.4 us (36%)
  waiting for transfers between devices  1.88 us (4%)
  between operations  1.36 us (3%)
    all_to_all x2, starting transfers between devices, shards(): lax.all_to_all(leaving, both, split_axis=0, concat_axis=0, tiled=True)  12.8 us
    pallas_call x1, Pallas kernels, shards(): pl.pallas_call(functools.partial(first_kernel, sz), out_shape=[pltpu.HBM(...  8.82 us
    pallas_call x1, Pallas kernels, shards(): pl.pallas_call(functools.partial(own_kernel, sz), out_shape=[so_far, so_f...  6.69 us
    pallas_call x1, Pallas kernels, shards(): pl.pallas_call(functools.partial(ghost_kernel, sz), out_shape=[result, re...  6.46 us
    ppermute x3, starting transfers between devices, swap(): return lax.ppermute(value, axis, [(d, d ^ k) for d in range(size)])  3.61 us
    pallas_call x1, Pallas kernels, shards(): pl.pallas_call(functools.partial(source_kernel, sz), out_shape=[shape(ben...  2.38 us
    all_to_all x2, waiting for transfers between devices, shards(): lax.all_to_all(leaving, both, split_axis=0, concat_axis=0, tiled=True)  1.87 us
    pallas_call x1, Pallas kernels, shards(): pl.pallas_call(functools.partial(pick_kernel, sz), out_shape=[slot_shape,...  1.85 us
  transfers between devices with their start and end apart: 5, of which 1 were waited for; matrix products, arithmetic and copies ran while one was open for 0% of the time, Pallas kernels for 20%

profile of v2, /device:TPU:25, one launch (start us, length us, event | category | flops | bytes accessed | tf_op | source)
XLA Modules:
  0.0 45.9 jit_solution(4981567809751229053)
XLA Ops:
  1.3 1.8 %pick_cells.1 = (f32[128,128]{1,0:T(8,128)}, s32[1,8]{1,0:T(1,128)}) custom-call(s32[1,8]{1,0:T(1,128)} %refs_0_.1, s32[1,12]{1,0:T(1,128)} %refs_1_.2, s32[1,12]{1,0:T(1,128)} %refs_2_.1, s32[1]{0:T(128)S(6)} %copy.8.refs_3_, f32[3,32,544]{2,1,0:T(8,128)} %bitcast.9), custom_call_target="tpu_custom_call" | custom-call | tf_op jit(solution)/shard_map/pick_cells/pallas_call | solution.py:733
  3.1 6.2 %all-to-all-start = ((f32[32,4,128]{2,1,0:T(4,128)}), f32[32,4,128]{2,1,0:T(4,128)S(1)}, u32[]{:S(2)}, u32[]{:S(2)}) async-start(f32[32,4,128]{2,1,0:T(4,128)} %bitcast.13), calls=%async_computation | async-start | bytes 131072 | tf_op jit(solution)/shard_map/all_to_all | solution.py:750
  9.3 2.4 %first_sources.1 = (bf16[544,544]{1,0:T(8,128)(2,1)S(1)}, bf16[544,544]{1,0:T(8,128)(2,1)S(1)}, f32[5,768,128]{2,1,0:T(8,128)S(1)}, f32[256,128]{1,0:T(8,128)S(1)}) custom-call(f32[3,32,544]{2,1,0:T(8,128)} %bitcast.10, f32[544,544]{1,0:T(8,128)} %refs_1_.3), custom_call_target="tpu_custom_call" | custom-call | flops 1000000000 | bytes 10000000 | tf_op jit(solution)/shard_map/first_sources/pallas_call | solution.py:751
  11.7 1.9 %all-to-all-done = f32[32,4,128]{2,1,0:T(4,128)S(1)} async-done(((f32[32,4,128]{2,1,0:T(4,128)}), f32[32,4,128]{2,1,0:T(4,128)S(1)}, u32[]{:S(2)}, u32[]{:S(2)}) %all-to-all-start) | async-done | bytes 65568 | tf_op jit(solution)/shard_map/all_to_all | solution.py:750
  13.6 8.8 %first_step.1 = (f32[104,128]{1,0:T(8,128)}, f32[128,128]{1,0:T(8,128)}, s32[3,64]{1,0:T(4,128)}) custom-call(f32[128,128]{1,0:T(8,128)S(1)} %bitcast.7, bf16[544,544]{1,0:T(8,128)(2,1)S(1)} %get-tuple-element.16.refs_1_.refs_0_, bf16[544,544]{1,0:T(8,128)(2,1)S(1)} %get-tuple-element.17.refs_2_.refs_1_, f32[5,768,128]{2,1,0:T(8,128)S(1)} %get-tuple-element.18.refs_3_, ...), custom_call_target="tpu_custom_call" | custom-call | tf_op jit(solution)/shard_map/first_step/pallas_call | solution.py:771
  22.4 2.7 %collective-permute-start.2 = (f32[104,128]{1,0:T(8,128)}, f32[104,128]{1,0:T(8,128)S(1)}, u32[]{:S(2)}, u32[]{:S(2)}) collective-permute-start(f32[104,128]{1,0:T(8,128)} %get-tuple-element.22.refs_6_), channel_id=1, source_target_pairs={{0,3},{1,2},{2,1},{3,0},{4,7},{5,6},{6,5},{7,4},{8,11},{9,10},{10,... | collective-permute-start | bytes 159752 | tf_op jit(solution)/shard_map/ppermute | solution.py:716
  25.1 0.0 collective-permute-start.1
  25.1 0.9 %collective-permute-start = (f32[104,128]{1,0:T(8,128)}, f32[104,128]{1,0:T(8,128)S(1)}, u32[]{:S(2)}, u32[]{:S(2)}) collective-permute-start(f32[104,128]{1,0:T(8,128)} %get-tuple-element.22.refs_6_), channel_id=1, source_target_pairs={{0,1},{1,0},{2,3},{3,2},{4,5},{5,4},{6,7},{7,6},{8,9},{9,8},{10,11... | collective-permute-start | bytes 159752 | tf_op jit(solution)/shard_map/ppermute | solution.py:716
  26.0 6.6 %all-to-all-start.1 = ((f32[32,4,128]{2,1,0:T(4,128)}), f32[32,4,128]{2,1,0:T(4,128)S(1)}, u32[]{:S(2)}, u32[]{:S(2)}) async-start(f32[32,4,128]{2,1,0:T(4,128)} %bitcast.12), calls=%async_computation.1 | async-start | bytes 131072 | tf_op jit(solution)/shard_map/all_to_all | solution.py:796
  32.7 0.0 collective-permute-done.2.refs_4_
  32.7 0.0 collective-permute-done.1.refs_3_
  32.7 0.0 collective-permute-done.refs_2_
  32.7 6.7 %second_own.1 = (f32[3,8,640]{2,1,0:T(8,128)S(1)}, f32[3,8,640]{2,1,0:T(8,128)S(1)}) custom-call(bf16[544,544]{1,0:T(8,128)(2,1)S(1)} %get-tuple-element.16.refs_1_.refs_0_, bf16[544,544]{1,0:T(8,128)(2,1)S(1)} %get-tuple-element.17.refs_2_.refs_1_, f32[104,128]{1,0:T(8,128)S(1)} %collective-permute-done.refs_2_, ...), custom_call_target="tpu_custom_call" | custom-call | flops 1000000000 | bytes 10000000 | tf_op jit(solution)/shard_map/second_own/pallas_call | solution.py:800
  39.4 0.0 all-to-all-done.1
  39.4 6.5 %second_ghosts.1 = (f32[3,8,544]{2,1,0:T(8,128)}, f32[3,8,544]{2,1,0:T(8,128)}) custom-call(f32[128,128]{1,0:T(8,128)S(1)} %bitcast.8, bf16[544,544]{1,0:T(8,128)(2,1)S(1)} %get-tuple-element.16.refs_1_.refs_0_, bf16[544,544]{1,0:T(8,128)(2,1)S(1)} %get-tuple-element.17.refs_2_.refs_1_, f32[3,8,640]{2,1,0:T(8,128)S(1)} %get-tuple-element.24.refs_3_, ...), custom_call_target="tpu_custom_call" | custom-call | tf_op jit(solution)/shard_map/second_ghosts/pallas_call | solution.py:819
Async XLA Ops:
  3.1 10.5 %all-to-all-start = ((f32[32,4,128]{2,1,0:T(4,128)}), f32[32,4,128]{2,1,0:T(4,128)S(1)}, u32[]{:S(2)}, u32[]{:S(2)}) async-start(f32[32,4,128]{2,1,0:T(4,128)} %bitcast.13), calls=%async_computation | async-start | bytes 131072 | tf_op jit(solution)/shard_map/all_to_all | solution.py:750
  22.4 10.2 %collective-permute-start.2 = (f32[104,128]{1,0:T(8,128)}, f32[104,128]{1,0:T(8,128)S(1)}, u32[]{:S(2)}, u32[]{:S(2)}) collective-permute-start(f32[104,128]{1,0:T(8,128)} %get-tuple-element.22.refs_6_), channel_id=1, source_target_pairs={{0,3},{1,2},{2,1},{3,0},{4,7},{5,6},{6,5},{7,4},{8,11},{9,10},{10,... | collective-permute-start | bytes 159752 | tf_op jit(solution)/shard_map/ppermute | solution.py:716
  25.1 7.6 %collective-permute-start.1 = (f32[104,128]{1,0:T(8,128)}, f32[104,128]{1,0:T(8,128)S(1)}, u32[]{:S(2)}, u32[]{:S(2)}) collective-permute-start(f32[104,128]{1,0:T(8,128)} %get-tuple-element.22.refs_6_), channel_id=1, source_target_pairs={{0,2},{1,3},{2,0},{3,1},{4,6},{5,7},{6,4},{7,5},{8,10},{9,11},{10,... | collective-permute-start | bytes 159752 | tf_op jit(solution)/shard_map/ppermute | solution.py:716
  25.1 7.6 %collective-permute-start = (f32[104,128]{1,0:T(8,128)}, f32[104,128]{1,0:T(8,128)S(1)}, u32[]{:S(2)}, u32[]{:S(2)}) collective-permute-start(f32[104,128]{1,0:T(8,128)} %get-tuple-element.22.refs_6_), channel_id=1, source_target_pairs={{0,1},{1,0},{2,3},{3,2},{4,5},{5,4},{6,7},{7,6},{8,9},{9,8},{10,11... | collective-permute-start | bytes 159752 | tf_op jit(solution)/shard_map/ppermute | solution.py:716
  26.0 13.4 %all-to-all-start.1 = ((f32[32,4,128]{2,1,0:T(4,128)}), f32[32,4,128]{2,1,0:T(4,128)S(1)}, u32[]{:S(2)}, u32[]{:S(2)}) async-start(f32[32,4,128]{2,1,0:T(4,128)} %bitcast.12), calls=%async_computation.1 | async-start | bytes 131072 | tf_op jit(solution)/shard_map/all_to_all | solution.py:796
